TPU v7x, 32 devices: a whole 2x2x4 slice. The times are simulated.
32 devices in a mesh: space: 8 (over y, x, core), tm: 4 (over z).
Axes of the slice: x: 2, y: 2, z: 4, core: 2. Of those that a mesh axis runs over, the one named last changes fastest.
Arguments:
- field: bfloat16 [114688, 1024], P('space', 'tm'), may hold values from -6 to 6
- sp_blocks: bfloat16 [896, 5, 128, 128], P('space'), may hold values from -0.25 to 0.25
- sp_cols: int32 [896, 5], P('space'), may hold values from 0 to 895, as said below
- sp_count: int32 [896], P('space'), may hold values from 1 to 5, as said below
- tm_factor: bfloat16 [1024, 1024], replicated, may hold values from -0.1875 to 0.1875
Outputs:
- scores: float32 [114688], P(('space', 'tm'))
Inputs may be any that keep to these rules, and one draw needn't show every extreme that they name: `sp_count`: live slots come first; some row block has 5 live slots. `sp_cols`: slot 0 of row block r names r. Live slots 1 and on name distinct blocks (r + d) mod 896 with 1 <= |d| <= 112. Slots that are not live name r.
All inputs are finite; a program needn't handle non-finite values.
Results may differ from a plain program's by a relative error of at most 0.00038.
Values may be sent and summed in bfloat16 or wider, within the bound.
A program may use at most 192 MiB of HBM per device.

v0:
```python
import jax
import jax.numpy as jnp
from jax import lax
from jax.sharding import PartitionSpec as P


def extended(cells, sides, width):
    for axis, dim in sides:
        count = lax.axis_size(axis)
        head = lax.slice_in_dim(cells, 0, width, axis=dim)
        tail = lax.slice_in_dim(cells, cells.shape[dim] - width, cells.shape[dim], axis=dim)
        cells = jnp.concatenate(
            [
                lax.ppermute(tail, axis, [(i, (i + 1) % count) for i in range(count)]),
                cells,
                lax.ppermute(head, axis, [((i + 1) % count, i) for i in range(count)]),
            ],
            axis=dim,
        )
    return cells


def on_device(field, sp_blocks, sp_cols, sp_count, tm_factor):
    blocks_dev = sp_cols.shape[0]
    slot_count = sp_cols.shape[1]
    block_size = sp_blocks.shape[2]
    slab_steps = field.shape[1]
    step_count = tm_factor.shape[0]
    node_count = blocks_dev * block_size
    total_blocks = blocks_dev * lax.axis_size("space")
    padded = extended(field, (("space", 0),), blocks_dev * block_size)
    padded_blocks = padded.reshape(3 * blocks_dev, block_size, slab_steps)
    row_index = lax.axis_index("space") * blocks_dev + jnp.arange(blocks_dev, dtype=jnp.int32)
    offset = jnp.mod(sp_cols - row_index[:, None] + blocks_dev, total_blocks)
    position = jnp.arange(blocks_dev, dtype=jnp.int32)[:, None] + offset
    alive_slot = jnp.arange(slot_count, dtype=jnp.int32)[None, :] < sp_count[:, None]
    zero_value = jnp.zeros((), jnp.bfloat16)
    picked = jnp.take(padded_blocks, position, axis=0)
    weights = jnp.where(alive_slot[:, :, None, None], sp_blocks, zero_value)
    spatial = jnp.einsum("rkab,rkbt->rat", weights, picked, preferred_element_type=jnp.float32)
    spatial = spatial.astype(jnp.bfloat16)
    spatial_flat = spatial.reshape(node_count, slab_steps)
    own_rows = lax.dynamic_slice_in_dim(tm_factor, lax.axis_index("tm") * slab_steps, slab_steps, 0)
    whitened = lax.psum_scatter(
        jnp.dot(spatial_flat, own_rows, preferred_element_type=jnp.float32),
        "tm",
        scatter_dimension=0,
        tiled=True,
    )
    scores = jnp.sum(whitened * whitened, axis=1) / step_count
    return scores


def solution(mesh):
    in_specs = (P("space", "tm"), P("space", None, None, None), P("space", None), P("space"), P())
    out_specs = P(("space", "tm"))
    return jax.shard_map(
        on_device, mesh=mesh, in_specs=in_specs, out_specs=out_specs, check_vma=False
    )
```

profile of v0, /device:TPU:0, one launch (start us, length us, event | category | flops | bytes accessed | tf_op | source)
XLA Modules:
  0.0 1243.7 jit_solution(10286980107313749872)
XLA Ops:
  6.5 0.0 copy-start
  6.5 0.0 reduce-scatter.2.cloned.1.call-start
  6.5 0.5 collective-permute-start
  7.0 2.9 collective-permute-start.1
  9.9 0.7 compare_and_fusion
  10.6 0.1 copy.7
  10.7 0.1 copy.8
  10.8 0.2 reshape.40
  11.0 0.7 iota_compare_fusion
  11.8 154.3 %collective-permute-done = bf16[14336,256]{1,0:T(8,128)(2,1)} collective-permute-done((bf16[14336,256]{1,0:T(8,128)(2,1)}, bf16[14336,256]{1,0:T(8,128)(2,1)}, u32[]{:S(2)}, u32[]{:S(2)}) %collective-permute-start) | collective-permute-done | bytes 7340064 | tf_op jit(solution)/shard_map/ppermute | solution.py:14
  166.1 1.5 collective-permute-done.1
  167.6 34.4 %pad_maximum_fusion = bf16[43008,256]{1,0:T(8,128)(2,1)} fusion(bf16[14336,256]{1,0:T(8,128)(2,1)} %collective-permute-done.1, bf16[14336,256]{1,0:T(8,128)(2,1)} %param.5, bf16[14336,256]{1,0:T(8,128)(2,1)} %collective-permute-done), kind=kLoop, calls=%fused_computation.4 | loop fusion | flops 66060288 | bytes 44040192 | tf_op jit(solution)/shard_map/concatenate | solution.py:12
  202.0 24.8 %gather_fusion = bf16[560,128,256]{2,1,0:T(8,128)(2,1)} fusion(bf16[336,128,256]{2,1,0:T(8,128)(2,1)} %bitcast.7, s32[1024]{0:T(1024)S(1)} %pad_clamp_fusion), kind=kCustom, calls=%fused_computation | custom fusion | bytes 73402560 | tf_op jit(solution)/shard_map/jit(_take)/gather | solution.py:38
  226.8 22.2 %bitcast_convert_fusion = bf16[112,128,256]{2,1,0:T(8,128)(2,1)} fusion(bf16[112,5,128,256]{3,2,1,0:T(8,128)(2,1)} %bitcast.8, pred[112,5]{1,0:T(8,128)(4,1)S(1)} %copy.7, bf16[112,5,128,128]{3,2,1,0:T(8,128)(2,1)} %param.6, pred[112,5]{1,0:T(8,128)(4,1)S(1)} %iota_compare_fusion), kind=kOutput, calls=%fused_computation.8 | convolution fusion | flops 4728815616 | bytes 62391392 | tf_op jit(solution)/shard_map/rkab,rkbt->rat/dot_general | solution.py:40
  249.0 0.0 copy-done
  249.0 23.5 %fusion.11 = f32[14336,1024]{1,0:T(8,128)} fusion(bf16[14336,256]{1,0:T(8,128)(2,1)} %bitcast.9, bf16[1024,1024]{1,0:T(8,128)(2,1)S(1)} %copy-done, s32[]{:T(128)S(6)} %select_n.27), kind=kOutput, calls=%fused_computation.11 | convolution fusion | flops 7516192768 | bytes 66584580 | tf_op jit(solution)/shard_map/dot_general | solution.py:45
  272.5 0.0 reduce-scatter.2.cloned.1.call-update
  272.5 957.5 %reduce-scatter.2.cloned.1.call-done = f32[3584,1024]{1,0:T(8,128)} async-done(((f32[14336,1024]{1,0:T(8,128)}), f32[3584,1024]{1,0:T(8,128)}) %reduce-scatter.2.cloned.1.call-update) | async-done | bytes 14680080 | tf_op jit(solution)/shard_map/reduce_scatter | solution.py:44
  1230.0 6.2 multiply_reduce_fusion
  1236.2 0.6 broadcast_multiply_fusion
  (2 shorter events, 0.0 us)
Async XLA Ops:
  6.5 242.4 %copy-start = (bf16[1024,1024]{1,0:T(8,128)(2,1)S(1)}, bf16[1024,1024]{1,0:T(8,128)(2,1)}, u32[]{:S(2)}) copy-start(bf16[1024,1024]{1,0:T(8,128)(2,1)} %param.9) | copy-start | bytes 6291460
  6.5 1223.5 %reduce-scatter.2.cloned.1.call-start = ((), (), s32[]{:S(2)}) async-start(), calls=%async_computation.1 | async-start | bytes 73400320 | tf_op jit(solution)/shard_map/reduce_scatter | solution.py:44
  6.5 159.5 %collective-permute-start = (bf16[14336,256]{1,0:T(8,128)(2,1)}, bf16[14336,256]{1,0:T(8,128)(2,1)}, u32[]{:S(2)}, u32[]{:S(2)}) collective-permute-start(bf16[14336,256]{1,0:T(8,128)(2,1)} %param.5), channel_id=1, source_target_pairs={{0,4},{4,8},{8,12},{12,16},{16,20},{20,24},{24,28},{28,0},{1,5},{5... | collective-permute-start | bytes 22020104 | tf_op jit(solution)/shard_map/ppermute | solution.py:14
  7.0 160.6 %collective-permute-start.1 = (bf16[14336,256]{1,0:T(8,128)(2,1)}, bf16[14336,256]{1,0:T(8,128)(2,1)}, u32[]{:S(2)}, u32[]{:S(2)}) collective-permute-start(bf16[14336,256]{1,0:T(8,128)(2,1)} %param.5), channel_id=1, source_target_pairs={{4,0},{8,4},{12,8},{16,12},{20,16},{24,20},{28,24},{0,28},{5,1},{9... | collective-permute-start | bytes 22020104 | tf_op jit(solution)/shard_map/ppermute | solution.py:16
Sparse Core Ops, SparseCore 0:
  272.6 957.3 reduce-scatter.1
where the time goes:
time: 1240 us
  waiting for transfers between devices  1110 us (90%)
  matrix products  45.7 us (4%)
  other arithmetic  42.7 us (3%)
  local copies, waits for them, and re-layouts  25.2 us (2%)
  between operations  13.4 us (1%)
    reduce_scatter x1, waiting for transfers between devices, on_device(): lax.psum_scatter(jnp.dot(spatial_flat, own_rows, preferred_element_type=j...  958 us
    ppermute x1, waiting for transfers between devices, extended(): lax.ppermute(tail, axis, [(i, (i + 1) % count) for i in range(count)])  154 us
    concatenate x1, other arithmetic, extended(): jnp.concatenate([lax.ppermute(tail, axis, [(i, (i + 1) % count) for i in...  34.4 us
  transfers between devices with their start and end apart: 3, of which 3 were waited for; matrix products, arithmetic and copies ran while one was open for 0% of the time, Pallas kernels for 0%

commit v1 on v0

v1 whole, which is shorter than its diff:
```python
import functools

import jax
import jax.numpy as jnp
from jax import lax
from jax.experimental import pallas as pl
from jax.experimental.pallas import tpu as pltpu
from jax.sharding import PartitionSpec as P

LANES = 128


def spatial_kernel(group, slots, block, pos_ref, blocks_ref, left_ref, own_ref, right_ref, out_ref, near, sems):
    nodes = own_ref.shape[0]
    step = pl.program_id(0)

    @pl.when(step == 0)
    def _():
        parts = (left_ref, own_ref, right_ref)
        copies = [
            pltpu.make_async_copy(part, near.at[pl.ds(i * nodes, nodes)], sems.at[i])
            for i, part in enumerate(parts)
        ]
        for copy in copies:
            copy.start()
        near[pl.ds(3 * nodes, block), :] = jnp.zeros((block, near.shape[1]), near.dtype)
        for copy in copies:
            copy.wait()

    for i in range(group):
        row = step * group + i
        weights = jnp.concatenate([blocks_ref[i, k] for k in range(slots)], axis=1)
        picked = jnp.concatenate(
            [near[pl.ds(pl.multiple_of(pos_ref[row * slots + k] * block, block), block), :] for k in range(slots)],
            axis=0,
        )
        out_ref[pl.ds(i * block, block), :] = jnp.dot(
            weights, picked, preferred_element_type=jnp.float32
        ).astype(out_ref.dtype)


def spatial_of(position, sp_blocks, left, own, right):
    blocks_dev, slots, block, _ = sp_blocks.shape
    nodes, width = own.shape
    group = 8
    any_spec = pl.BlockSpec(memory_space=pl.ANY)
    return pl.pallas_call(
        functools.partial(spatial_kernel, group, slots, block),
        out_shape=jax.ShapeDtypeStruct((nodes, width), jnp.bfloat16),
        grid_spec=pltpu.PrefetchScalarGridSpec(
            num_scalar_prefetch=1,
            grid=(blocks_dev // group,),
            in_specs=[
                pl.BlockSpec((group, slots, block, block), lambda g, *_: (g, 0, 0, 0)),
                any_spec,
                any_spec,
                any_spec,
            ],
            out_specs=pl.BlockSpec((group * block, width), lambda g, *_: (g, 0)),
            scratch_shapes=[
                pltpu.VMEM((3 * nodes + block, width), jnp.bfloat16),
                pltpu.SemaphoreType.DMA((3,)),
            ],
        ),
        compiler_params=pltpu.CompilerParams(vmem_limit_bytes=32 << 20),
        cost_estimate=pl.CostEstimate(
            flops=2 * nodes * block * slots * width,
            bytes_accessed=2 * sp_blocks.size + 8 * nodes * width,
            transcendentals=0,
        ),
    )(position, sp_blocks, left, own, right)


def score_kernel(sources, chunks, slab, src_ref, factor_ref, *refs):
    pieces, out_ref = refs[:-1], refs[-1]
    steps = factor_ref.shape[0]
    tile = pieces[0].shape[0]
    total = None
    for s in range(sources):
        cells = jnp.concatenate([pieces[s * chunks + c][...] for c in range(chunks)], axis=1)
        rows = factor_ref[pl.ds(pl.multiple_of(src_ref[s] * slab, slab), slab), :]
        part = jnp.dot(cells, rows, preferred_element_type=jnp.float32)
        total = part if total is None else total + part
    square = total * total
    folded = square[:, :LANES]
    for c in range(1, steps // LANES):
        folded = folded + square[:, c * LANES : (c + 1) * LANES]
    for j in range(tile // LANES):
        column = jnp.sum(folded[j * LANES : (j + 1) * LANES, :].T, axis=0, keepdims=True)
        out_ref[pl.ds(pl.program_id(0) * (tile // LANES) + j, 1), :] = column / steps


def scores_of(src, tm_factor, pieces, slab):
    rows, width = pieces[0].shape
    chunks = slab // width
    steps = tm_factor.shape[0]
    tile = 256
    out = pl.pallas_call(
        functools.partial(score_kernel, len(pieces) // chunks, chunks, slab),
        out_shape=jax.ShapeDtypeStruct((rows // LANES, LANES), jnp.float32),
        grid_spec=pltpu.PrefetchScalarGridSpec(
            num_scalar_prefetch=1,
            grid=(rows // tile,),
            in_specs=[pl.BlockSpec((steps, steps), lambda g, *_: (0, 0))]
            + [pl.BlockSpec((tile, width), lambda g, *_: (g, 0))] * len(pieces),
            out_specs=pl.BlockSpec((rows // LANES, LANES), lambda g, *_: (0, 0)),
        ),
        compiler_params=pltpu.CompilerParams(vmem_limit_bytes=32 << 20),
        cost_estimate=pl.CostEstimate(
            flops=2 * rows * steps * steps, bytes_accessed=2 * rows * steps + 2 * steps * steps, transcendentals=0
        ),
    )(src, tm_factor, *pieces)
    return out.reshape(rows)


def on_device(field, sp_blocks, sp_cols, sp_count, tm_factor):
    blocks_dev, slots = sp_cols.shape
    slab = field.shape[1]
    space_count, tm_count = lax.axis_size("space"), lax.axis_size("tm")
    total_blocks = blocks_dev * space_count
    local = jnp.arange(blocks_dev, dtype=jnp.int32)[:, None]
    row_index = lax.axis_index("space") * blocks_dev + local
    position = local + jnp.mod(sp_cols - row_index + blocks_dev, total_blocks)
    alive = jnp.arange(slots, dtype=jnp.int32)[None, :] < sp_count[:, None]
    position = jnp.where(alive, position, 3 * blocks_dev).reshape(-1)

    up = [(i, (i + 1) % space_count) for i in range(space_count)]
    down = [((i + 1) % space_count, i) for i in range(space_count)]
    me = lax.axis_index("tm")
    rows = field.shape[0] // tm_count
    chunks = slab // LANES
    received = [[None] * chunks for _ in range(tm_count)]
    left = right = None
    for c in range(chunks):
        own = lax.slice_in_dim(field, c * LANES, (c + 1) * LANES, axis=1)
        if left is not None:
            own, left, right = lax.optimization_barrier((own, left, right))
        new_left = lax.ppermute(own, "space", up)
        new_right = lax.ppermute(own, "space", down)
        left, right = new_left, new_right
        spatial = spatial_of(position, sp_blocks, left, own, right)
        for k in range(tm_count):
            target = lax.rem(me + k, tm_count)
            piece = lax.dynamic_slice_in_dim(spatial, target * rows, rows, 0)
            if k:
                piece = lax.ppermute(piece, "tm", [(i, (i + k) % tm_count) for i in range(tm_count)])
            received[k][c] = piece
    src = jnp.stack([lax.rem(me - k + tm_count, tm_count) for k in range(tm_count)]).astype(jnp.int32)
    return scores_of(src, tm_factor, [p for group in received for p in group], slab)


def solution(mesh):
    in_specs = (P("space", "tm"), P("space", None, None, None), P("space", None), P("space"), P())
    out_specs = P(("space", "tm"))
    return jax.shard_map(
        on_device, mesh=mesh, in_specs=in_specs, out_specs=out_specs, check_vma=False
    )
```

time: 1240 us -> 294 us (0.24)
  waiting for transfers between devices: 1110 us -> 207 us
  Pallas kernels: 0 us -> 48.4 us
  matrix products: 45.7 us -> 0 us
  other arithmetic: 42.7 us -> 0.1 us
  between operations: 13.4 us -> 0.09 us
    reduce_scatter x1 -> x0, waiting for transfers between devices: 958 us -> none  [on_device(): lax.psum_scatter(jnp.dot(spatial_flat, own_rows, preferred_element_type=j...]
    ppermute x2 -> x10, waiting for transfers between devices: 156 us -> 207 us  [the longest x2 127 us: on_device(): new_right = lax.ppermute(own, 'space', down)]
    pallas_call x0 -> x3, Pallas kernels: none -> 48.4 us  [the longest x2 34 us: spatial_of(): pl.pallas_call(functools.partial(spatial_kernel, group, slots, block), ou...]
    dot_general x2 -> x0, matrix products: 45.7 us -> none  [the longest x1 23.5 us: on_device(): jnp.dot(spatial_flat, own_rows, preferred_element_type=jnp.float32)]
    concatenate x1 -> x0, other arithmetic: 34.4 us -> none  [extended(): jnp.concatenate([lax.ppermute(tail, axis, [(i, (i + 1) % count) for i in...]
    gather x1 -> x0, local copies, waits for them, and re-layouts: 24.8 us -> none  [on_device(): picked = jnp.take(padded_blocks, position, axis=0)]
    unnamed x2 -> x18, local copies, waits for them, and re-layouts: 0.01 us -> 13.3 us
  transfers between devices with their start and end apart: 3 -> 10, of which waited for: 3 -> 7; matrix products, arithmetic and copies ran while one was open for 0% -> 1% of each run, Pallas kernels for 0% -> 12%
where the time goes in v1:
time: 294 us; the launch traced here: 292 us
  waiting for transfers between devices  207 us (70%)
  Pallas kernels  48.4 us (16%)
  local copies, waits for them, and re-layouts  21.3 us (7%)
  starting transfers between devices  15.2 us (5%)
    ppermute x2, waiting for transfers between devices, on_device(): new_right = lax.ppermute(own, 'space', down)  127 us
    ppermute x6, waiting for transfers between devices, on_device(): lax.ppermute(piece, 'tm', [(i, (i + k) % tm_count) for i in range(tm_coun...  77.8 us
    pallas_call x2, Pallas kernels, spatial_of(): pl.pallas_call(functools.partial(spatial_kernel, group, slots, block), ou...  34 us
    pallas_call x1, Pallas kernels, scores_of(): pl.pallas_call(functools.partial(score_kernel, len(pieces) // chunks, chu...  14.5 us
    unnamed x18, local copies, waits for them, and re-layouts  13.3 us
    ppermute x6, starting transfers between devices, on_device(): lax.ppermute(piece, 'tm', [(i, (i + k) % tm_count) for i in range(tm_coun...  9.23 us
    ppermute x2, starting transfers between devices, on_device(): new_right = lax.ppermute(own, 'space', down)  6.01 us
  transfers between devices with their start and end apart: 10, of which 7 were waited for; matrix products, arithmetic and copies ran while one was open for 1% of the time, Pallas kernels for 12%

profile of v1, /device:TPU:0, one launch (start us, length us, event | category | flops | bytes accessed | tf_op | source)
XLA Modules:
  0.0 291.8 jit_solution(4050977725052816621)
XLA Ops:
  0.0 0.0 copy-start.8
  0.0 0.0 copy-start.7
  0.0 4.6 %fusion.2 = (bf16[14336,128]{1,0:T(8,128)(2,1)}, bf16[14336,128]{1,0:T(8,128)(2,1)S(1)}) fusion(bf16[14336,256]{1,0:T(8,128)(2,1)} %param.5), kind=kLoop, calls=%fused_computation.15 | loop fusion | bytes 14680064 | tf_op jit(solution)/shard_map/slice | solution.py:135
  4.6 3.3 %collective-permute-start.1 = (bf16[14336,128]{1,0:T(8,128)(2,1)S(1)}, bf16[14336,128]{1,0:T(8,128)(2,1)S(1)}, u32[]{:S(2)}, u32[]{:S(2)}) collective-permute-start(bf16[14336,128]{1,0:T(8,128)(2,1)S(1)} %get-tuple-element.8.own_ref), channel_id=1, source_target_pairs={{4,0},{8,4},{12,8},{16,12},{20,16},{24,20},{28,24},{0,28},{5,1},{9... | collective-permute-start | bytes 11010056 | tf_op jit(solution)/shard_map/ppermute | solution.py:139
  8.0 0.0 collective-permute-start
  8.0 0.0 copy-start
  8.0 1.8 copy-done
  9.8 77.0 %collective-permute-done.1.right_ref = bf16[14336,128]{1,0:T(8,128)(2,1)S(1)} collective-permute-done((bf16[14336,128]{1,0:T(8,128)(2,1)S(1)}, bf16[14336,128]{1,0:T(8,128)(2,1)S(1)}, u32[]{:S(2)}, u32[]{:S(2)}) %collective-permute-start.1) | collective-permute-done | bytes 3670048 | tf_op jit(solution)/shard_map/ppermute | solution.py:139
  86.7 0.0 copy-start.2
  86.7 1.8 copy-done.2
  88.6 0.1 collective-permute-done.left_ref
  88.7 0.0 copy-start.4
  88.7 1.9 copy-done.4
  90.6 2.7 collective-permute-start.3
  93.3 0.0 collective-permute-start.2
  93.3 0.0 copy-done.8
  93.3 0.0 copy-done.7
  93.3 0.1 copy.6
  93.4 0.2 reshape.12.pos_ref
  93.7 0.0 copy-start.1
  93.7 2.0 copy-done.1
  95.7 0.0 copy-start.3
  95.7 2.0 copy-done.3
  97.7 0.0 copy-start.5
  97.7 2.0 copy-done.5
  99.8 15.2 %shard_map.55 = bf16[14336,128]{1,0:T(8,128)(2,1)S(1)} custom-call(s32[560]{0:T(1024)S(1)} %reshape.12.pos_ref, bf16[112,5,128,128]{3,2,1,0:T(8,128)(2,1)} %blocks_ref.3, bf16[14336,128]{1,0:T(8,128)(2,1)S(1)} %copy-done.5, bf16[14336,128]{1,0:T(8,128)(2,1)S(1)} %copy-done.1, bf16[14336,128]{1,0:T(8,128)(2,1)S(1)} %copy-done.3), custom_call_target="tpu_custom_call" | custom-call | flops 2348810240 | bytes 33030144 | tf_op jit(solution)/shard_map/pallas_call | solution.py:47
  115.0 1.5 constant_dynamic-slice_fusion.1
  116.5 3.6 %collective-permute-start.8 = (bf16[3584,128]{1,0:T(8,128)(2,1)S(1)}, bf16[3584,128]{1,0:T(8,128)(2,1)S(1)}, u32[]{:S(2)}, u32[]{:S(2)}) collective-permute-start(bf16[3584,128]{1,0:T(8,128)(2,1)S(1)} %get-tuple-element.13), channel_id=1, source_target_pairs={{0,3},{1,0},{2,1},{3,2},{4,7},{5,4},{6,5},{7,6},{8,11},{9,8},{10,9... | collective-permute-start | bytes 2752520 | tf_op jit(solution)/shard_map/ppermute | solution.py:146
  120.1 0.0 collective-permute-start.6
  120.1 1.0 collective-permute-start.4
  121.1 49.8 %collective-permute-done.3.right_ref = bf16[14336,128]{1,0:T(8,128)(2,1)} collective-permute-done((bf16[14336,128]{1,0:T(8,128)(2,1)}, bf16[14336,128]{1,0:T(8,128)(2,1)}, u32[]{:S(2)}, u32[]{:S(2)}) %collective-permute-start.3) | collective-permute-done | bytes 3670048 | tf_op jit(solution)/shard_map/ppermute | solution.py:139
  170.9 2.0 collective-permute-done.2.left_ref
  172.9 18.8 %shard_map.56 = bf16[14336,128]{1,0:T(8,128)(2,1)S(1)} custom-call(s32[560]{0:T(1024)S(1)} %reshape.12.pos_ref, bf16[112,5,128,128]{3,2,1,0:T(8,128)(2,1)} %blocks_ref.3, bf16[14336,128]{1,0:T(8,128)(2,1)} %collective-permute-done.2.left_ref, bf16[14336,128]{1,0:T(8,128)(2,1)} %get-tuple-element.6.own_ref, bf16[14336,128]{1,0:T(8,128)(2,1)} %collective-permute-done.3.right_ref), custom_call_target="tpu_custom_call" | custom-call | flops 2348810240 | bytes 33030144 | tf_op jit(solution)/shard_map/pallas_call | solution.py:47
  191.6 1.6 constant_dynamic-slice_fusion
  193.3 3.6 %collective-permute-start.9 = (bf16[3584,128]{1,0:T(8,128)(2,1)}, bf16[3584,128]{1,0:T(8,128)(2,1)}, u32[]{:S(2)}, u32[]{:S(2)}) collective-permute-start(bf16[3584,128]{1,0:T(8,128)(2,1)} %get-tuple-element.9), channel_id=1, source_target_pairs={{0,3},{1,0},{2,1},{3,2},{4,7},{5,4},{6,5},{7,6},{8,11},{9,8},{10,9... | collective-permute-start | bytes 2752520 | tf_op jit(solution)/shard_map/ppermute | solution.py:146
  196.9 0.0 collective-permute-start.7
  196.9 0.0 collective-permute-done.8.refs_6_
  196.9 1.0 collective-permute-start.5
  197.9 0.1 pad_add_fusion.src_ref
  198.0 2.0 collective-permute-done.6.refs_4_
  199.9 0.0 collective-permute-done.4.refs_2_
  199.9 18.1 %collective-permute-done.9.refs_7_ = bf16[3584,128]{1,0:T(8,128)(2,1)} collective-permute-done((bf16[3584,128]{1,0:T(8,128)(2,1)}, bf16[3584,128]{1,0:T(8,128)(2,1)}, u32[]{:S(2)}, u32[]{:S(2)}) %collective-permute-start.9) | collective-permute-done | bytes 917536 | tf_op jit(solution)/shard_map/ppermute | solution.py:146
  218.0 57.8 %collective-permute-done.7.refs_5_ = bf16[3584,128]{1,0:T(8,128)(2,1)} collective-permute-done((bf16[3584,128]{1,0:T(8,128)(2,1)}, bf16[3584,128]{1,0:T(8,128)(2,1)}, u32[]{:S(2)}, u32[]{:S(2)}) %collective-permute-start.7) | collective-permute-done | bytes 917536 | tf_op jit(solution)/shard_map/ppermute | solution.py:146
  275.8 0.0 collective-permute-done.5.refs_3_
  275.8 0.0 copy-start.6
  275.8 1.6 copy-done.6
  277.3 14.5 %shard_map.57 = f32[28,128]{1,0:T(8,128)} custom-call(s32[4]{0:T(128)S(1)} %pad_add_fusion.src_ref, bf16[1024,1024]{1,0:T(8,128)(2,1)S(1)} %copy-done.6, bf16[3584,128]{1,0:T(8,128)(2,1)S(1)} %get-tuple-element.16.refs_0_, bf16[3584,128]{1,0:T(8,128)(2,1)S(1)} %get-tuple-element.12.refs_1_, bf16[3584,128]{1,0:T(8,128)(2,1)} %collective-permute-done.4.refs_2_, ...), custom_call_target="tpu_custom_call" | custom-call | flops 7516192768 | bytes 9437184 | tf_op jit(solution)/shard_map/pallas_call | solution.py:98
  (2 shorter events, 0.0 us)
Async XLA Ops:
  0.0 93.3 %copy-start.8 = (s32[112]{0:T(128)S(1)}, s32[112]{0:T(128)}, u32[]{:S(2)}) copy-start(s32[112]{0:T(128)} %param.8) | copy-start | bytes 1348
  0.0 93.3 %copy-start.7 = (s32[112,5]{0,1:T(8,128)S(1)}, s32[112,5]{0,1:T(8,128)}, u32[]{:S(2)}) copy-start(s32[112,5]{0,1:T(8,128)} %param.7) | copy-start | bytes 6724
  4.6 82.1 %collective-permute-start.1 = (bf16[14336,128]{1,0:T(8,128)(2,1)S(1)}, bf16[14336,128]{1,0:T(8,128)(2,1)S(1)}, u32[]{:S(2)}, u32[]{:S(2)}) collective-permute-start(bf16[14336,128]{1,0:T(8,128)(2,1)S(1)} %get-tuple-element.8.own_ref), channel_id=1, source_target_pairs={{4,0},{8,4},{12,8},{16,12},{20,16},{24,20},{28,24},{0,28},{5,1},{9... | collective-permute-start | bytes 11010056 | tf_op jit(solution)/shard_map/ppermute | solution.py:139
  8.0 80.7 %collective-permute-start = (bf16[14336,128]{1,0:T(8,128)(2,1)S(1)}, bf16[14336,128]{1,0:T(8,128)(2,1)S(1)}, u32[]{:S(2)}, u32[]{:S(2)}) collective-permute-start(bf16[14336,128]{1,0:T(8,128)(2,1)S(1)} %get-tuple-element.8.own_ref), channel_id=1, source_target_pairs={{0,4},{4,8},{8,12},{12,16},{16,20},{20,24},{24,28},{28,0},{1,5},{5... | collective-permute-start | bytes 11010056 | tf_op jit(solution)/shard_map/ppermute | solution.py:138
  8.0 1.8 copy-start
  86.7 1.8 copy-start.2
  88.7 1.9 copy-start.4
  90.6 80.3 %collective-permute-start.3 = (bf16[14336,128]{1,0:T(8,128)(2,1)}, bf16[14336,128]{1,0:T(8,128)(2,1)}, u32[]{:S(2)}, u32[]{:S(2)}) collective-permute-start(bf16[14336,128]{1,0:T(8,128)(2,1)} %get-tuple-element.6.own_ref), channel_id=1, source_target_pairs={{4,0},{8,4},{12,8},{16,12},{20,16},{24,20},{28,24},{0,28},{5,1},{9... | collective-permute-start | bytes 11010056 | tf_op jit(solution)/shard_map/ppermute | solution.py:139
  93.3 79.6 %collective-permute-start.2 = (bf16[14336,128]{1,0:T(8,128)(2,1)}, bf16[14336,128]{1,0:T(8,128)(2,1)}, u32[]{:S(2)}, u32[]{:S(2)}) collective-permute-start(bf16[14336,128]{1,0:T(8,128)(2,1)} %get-tuple-element.6.own_ref), channel_id=1, source_target_pairs={{0,4},{4,8},{8,12},{12,16},{16,20},{20,24},{24,28},{28,0},{1,5},{5... | collective-permute-start | bytes 11010056 | tf_op jit(solution)/shard_map/ppermute | solution.py:138
  93.7 2.0 copy-start.1
  95.7 2.0 copy-start.3
  97.7 2.0 copy-start.5
  116.5 80.4 %collective-permute-start.8 = (bf16[3584,128]{1,0:T(8,128)(2,1)S(1)}, bf16[3584,128]{1,0:T(8,128)(2,1)S(1)}, u32[]{:S(2)}, u32[]{:S(2)}) collective-permute-start(bf16[3584,128]{1,0:T(8,128)(2,1)S(1)} %get-tuple-element.13), channel_id=1, source_target_pairs={{0,3},{1,0},{2,1},{3,2},{4,7},{5,4},{6,5},{7,6},{8,11},{9,8},{10,9... | collective-permute-start | bytes 2752520 | tf_op jit(solution)/shard_map/ppermute | solution.py:146
  120.1 79.8 %collective-permute-start.6 = (bf16[3584,128]{1,0:T(8,128)(2,1)}, bf16[3584,128]{1,0:T(8,128)(2,1)}, u32[]{:S(2)}, u32[]{:S(2)}) collective-permute-start(bf16[3584,128]{1,0:T(8,128)(2,1)} %get-tuple-element.14), channel_id=1, source_target_pairs={{0,2},{1,3},{2,0},{3,1},{4,6},{5,7},{6,4},{7,5},{8,10},{9,11},{10,... | collective-permute-start | bytes 2752520 | tf_op jit(solution)/shard_map/ppermute | solution.py:146
  120.1 79.8 %collective-permute-start.4 = (bf16[3584,128]{1,0:T(8,128)(2,1)}, bf16[3584,128]{1,0:T(8,128)(2,1)}, u32[]{:S(2)}, u32[]{:S(2)}) collective-permute-start(bf16[3584,128]{1,0:T(8,128)(2,1)} %get-tuple-element.15), channel_id=1, source_target_pairs={{0,1},{1,2},{2,3},{3,0},{4,5},{5,6},{6,7},{7,4},{8,9},{9,10},{10,1... | collective-permute-start | bytes 2752520 | tf_op jit(solution)/shard_map/ppermute | solution.py:146
  193.3 24.7 %collective-permute-start.9 = (bf16[3584,128]{1,0:T(8,128)(2,1)}, bf16[3584,128]{1,0:T(8,128)(2,1)}, u32[]{:S(2)}, u32[]{:S(2)}) collective-permute-start(bf16[3584,128]{1,0:T(8,128)(2,1)} %get-tuple-element.9), channel_id=1, source_target_pairs={{0,3},{1,0},{2,1},{3,2},{4,7},{5,4},{6,5},{7,6},{8,11},{9,8},{10,9... | collective-permute-start | bytes 2752520 | tf_op jit(solution)/shard_map/ppermute | solution.py:146
  196.9 78.9 %collective-permute-start.7 = (bf16[3584,128]{1,0:T(8,128)(2,1)}, bf16[3584,128]{1,0:T(8,128)(2,1)}, u32[]{:S(2)}, u32[]{:S(2)}) collective-permute-start(bf16[3584,128]{1,0:T(8,128)(2,1)} %get-tuple-element.10), channel_id=1, source_target_pairs={{0,2},{1,3},{2,0},{3,1},{4,6},{5,7},{6,4},{7,5},{8,10},{9,11},{10,... | collective-permute-start | bytes 2752520 | tf_op jit(solution)/shard_map/ppermute | solution.py:146
  196.9 78.9 %collective-permute-start.5 = (bf16[3584,128]{1,0:T(8,128)(2,1)}, bf16[3584,128]{1,0:T(8,128)(2,1)}, u32[]{:S(2)}, u32[]{:S(2)}) collective-permute-start(bf16[3584,128]{1,0:T(8,128)(2,1)} %get-tuple-element.11), channel_id=1, source_target_pairs={{0,1},{1,2},{2,3},{3,0},{4,5},{5,6},{6,7},{7,4},{8,9},{9,10},{10,1... | collective-permute-start | bytes 2752520 | tf_op jit(solution)/shard_map/ppermute | solution.py:146
  275.8 1.6 copy-start.6

commit v2 on v0

v2 whole, which is shorter than its diff:
```python
import functools

import jax
import jax.numpy as jnp
from jax import lax
from jax.experimental import pallas as pl
from jax.experimental.pallas import tpu as pltpu
from jax.sharding import PartitionSpec as P

LANES = 128
PIECES = 8
AHEAD = 3
MESH = pl.DeviceIdType.MESH


def kernel(dims, field_ref, blocks_ref, pos_ref, factor_ref, out_ref, *scratch):
    blocks_dev, slots, block, chunks, space_count, tm_count = dims
    near = scratch[:chunks]
    (land, blocks_buf, spatial, received, factor,
     own_sems, fast_send, fast_recv, slow_send, slow_recv,
     blocks_sems, z_send, z_recv, local_sem, factor_sem) = scratch[chunks:]
    piece_blocks = blocks_dev // PIECES
    piece = piece_blocks * block
    steps_all = chunks * PIECES
    per_tm = PIECES // tm_count
    slab = chunks * LANES

    place = lax.axis_index("space")
    me = lax.axis_index("tm")
    odd = lax.rem(place, 2)
    sibling = place + 1 - 2 * odd
    far = lax.rem(place + 2 * odd - 1 + space_count, space_count)

    def ordered(g, first_up, count):
        return first_up * g + (1 - first_up) * (count - 1 - g)

    barrier = pltpu.get_barrier_semaphore()
    for other in (sibling, far):
        pl.semaphore_signal(barrier, inc=1, device_id=(other, me), device_id_type=MESH)
    for k in range(1, tm_count):
        pl.semaphore_signal(
            barrier, inc=1, device_id=(place, lax.rem(me + k, tm_count)), device_id_type=MESH
        )
    pl.semaphore_wait(barrier, tm_count + 1)

    def slow_copy(n):
        g, c = lax.rem(n, PIECES), n // PIECES
        start = ordered(g, 1 - odd, PIECES) * piece_blocks
        return pltpu.make_async_remote_copy(
            src_ref=field_ref.at[pl.ds(start, piece_blocks), :, pl.ds(pl.multiple_of(c * LANES, LANES), LANES)],
            dst_ref=land.at[n],
            send_sem=slow_send.at[n],
            recv_sem=slow_recv.at[n],
            device_id=(far, me),
            device_id_type=MESH,
        )

    def fast_copy(c):
        return pltpu.make_async_remote_copy(
            src_ref=field_ref.at[:, :, pl.ds(c * LANES, LANES)],
            dst_ref=near[c].at[pl.ds(odd * (2 * blocks_dev), blocks_dev)],
            send_sem=fast_send.at[c],
            recv_sem=fast_recv.at[c],
            device_id=(sibling, me),
            device_id_type=MESH,
        )

    def own_copy(c):
        return pltpu.make_async_copy(
            field_ref.at[:, :, pl.ds(c * LANES, LANES)], near[c].at[pl.ds(blocks_dev, blocks_dev)], own_sems.at[c]
        )

    def blocks_copy(n):
        start = ordered(lax.rem(n, PIECES), odd, PIECES) * piece_blocks
        slot = lax.rem(n, 2)
        return pltpu.make_async_copy(
            blocks_ref.at[pl.ds(start, piece_blocks)], blocks_buf.at[slot], blocks_sems.at[slot]
        )

    def target_of(g):
        p = ordered(g, odd, PIECES)
        return p, p // per_tm, lax.rem(p, per_tm)

    def z_copy(c, g):
        p, target, half = target_of(g)
        return pltpu.make_async_remote_copy(
            src_ref=spatial.at[c * PIECES + p],
            dst_ref=received.at[(me * chunks + c) * per_tm + half],
            send_sem=z_send.at[c * PIECES + g],
            recv_sem=z_recv.at[(me * chunks + c) * per_tm + half],
            device_id=(place, target),
            device_id_type=MESH,
        )

    slow_copy(0).start()
    fast_copy(0).start()
    for n in range(1, AHEAD):
        slow_copy(n).start()
    for c in range(chunks):
        own_copy(c).start()
    blocks_copy(0).start()
    factor_copy = pltpu.make_async_copy(factor_ref, factor, factor_sem)
    factor_copy.start()
    for c in range(chunks):
        near[c][3 * blocks_dev] = jnp.zeros((block, LANES), jnp.bfloat16)

    for c in range(chunks):
        own_copy(c).wait()
        fast_copy(c).wait()
        if c + 1 < chunks:
            fast_copy(c + 1).start()

        def stage(g, carry):
            n = c * PIECES + g
            p, target, half = target_of(g)

            @pl.when(n + 1 < steps_all)
            def _():
                blocks_copy(n + 1).start()

            arriving = slow_copy(n)
            arriving.wait_recv()
            arriving.wait_send()

            @pl.when(n + AHEAD < steps_all)
            def _():
                slow_copy(n + AHEAD).start()

            near[c][pl.ds(odd * (2 * blocks_dev) + p * piece_blocks, piece_blocks)] = land[n]
            blocks_copy(n).wait()
            slot = lax.rem(n, 2)

            def row(i, carry):
                base = (p * piece_blocks + i) * slots
                weights = jnp.concatenate([blocks_buf[slot, i, k] for k in range(slots)], axis=1)
                picked = jnp.concatenate(
                    [near[c][pos_ref[base + k]] for k in range(slots)], axis=0
                )
                spatial[c * PIECES + p, pl.ds(pl.multiple_of(i * block, block), block), :] = jnp.dot(
                    weights, picked, preferred_element_type=jnp.float32
                ).astype(jnp.bfloat16)
                return carry

            lax.fori_loop(0, piece_blocks, row, 0, unroll=2)

            @pl.when(target != me)
            def _():
                z_copy(c, g).start()

            @pl.when(target == me)
            def _():
                keep = pltpu.make_async_copy(
                    spatial.at[c * PIECES + p], received.at[(me * chunks + c) * per_tm + half], local_sem
                )
                keep.start()
                keep.wait()

            return carry

        lax.fori_loop(0, PIECES, stage, 0)

    factor_copy.wait()
    tile = 256
    width = factor.shape[0]
    for k in range(per_tm):
        half = ordered(k, odd, per_tm)
        for s in range(tm_count):

            @pl.when(me != s)
            def _():
                for c in range(chunks):
                    slot = (s * chunks + c) * per_tm + half
                    pltpu.make_async_remote_copy(
                        src_ref=received.at[slot],
                        dst_ref=received.at[slot],
                        send_sem=z_send.at[0],
                        recv_sem=z_recv.at[slot],
                        device_id=(place, s),
                        device_id_type=MESH,
                    ).wait_recv()

        def score(t, carry):
            rows = pl.ds(pl.multiple_of(t * tile, tile), tile)
            total = None
            for s in range(tm_count):
                cells = jnp.concatenate(
                    [received[(s * chunks + c) * per_tm + half, rows, :] for c in range(chunks)], axis=1
                )
                part = jnp.dot(cells, factor[s * slab : (s + 1) * slab, :], preferred_element_type=jnp.float32)
                total = part if total is None else total + part
            square = total * total
            folded = square[:, :LANES]
            for c in range(1, width // LANES):
                folded = folded + square[:, c * LANES : (c + 1) * LANES]
            for j in range(tile // LANES):
                column = jnp.sum(folded[j * LANES : (j + 1) * LANES, :].T, axis=0, keepdims=True)
                out_ref[pl.ds(half * (piece // LANES) + t * (tile // LANES) + j, 1), :] = column / width
            return carry

        lax.fori_loop(0, piece // tile, score, 0)

    for c in range(chunks):

        def finish(g, carry):
            _, target, _ = target_of(g)

            @pl.when(target != me)
            def _():
                z_copy(c, g).wait_send()

            return carry

        lax.fori_loop(0, PIECES, finish, 0)


def on_device(field, sp_blocks, sp_cols, sp_count, tm_factor):
    blocks_dev, slots, block, _ = sp_blocks.shape
    nodes, slab = field.shape
    space_count, tm_count = lax.axis_size("space"), lax.axis_size("tm")
    total_blocks = blocks_dev * space_count
    chunks = slab // LANES
    local = jnp.arange(blocks_dev, dtype=jnp.int32)[:, None]
    row_index = lax.axis_index("space") * blocks_dev + local
    position = local + jnp.mod(sp_cols - row_index + blocks_dev, total_blocks)
    alive = jnp.arange(slots, dtype=jnp.int32)[None, :] < sp_count[:, None]
    position = jnp.where(alive, position, 3 * blocks_dev).reshape(-1)

    piece = nodes // PIECES
    rows = nodes // tm_count
    per_tm = PIECES // tm_count
    steps_all = chunks * PIECES
    any_spec = pl.BlockSpec(memory_space=pl.ANY)
    dma = pltpu.SemaphoreType.DMA
    out = pl.pallas_call(
        functools.partial(kernel, (blocks_dev, slots, block, chunks, space_count, tm_count)),
        out_shape=jax.ShapeDtypeStruct((rows // LANES, LANES), jnp.float32),
        in_specs=[any_spec, any_spec, pl.BlockSpec(memory_space=pltpu.SMEM), any_spec],
        out_specs=pl.BlockSpec(memory_space=pltpu.VMEM),
        scratch_shapes=[pltpu.VMEM((3 * blocks_dev + 1, block, LANES), jnp.bfloat16) for _ in range(chunks)]
        + [
            pltpu.VMEM((steps_all, piece // block, block, LANES), jnp.bfloat16),
            pltpu.VMEM((2, blocks_dev // PIECES, slots, block, block), jnp.bfloat16),
            pltpu.VMEM((steps_all, piece, LANES), jnp.bfloat16),
            pltpu.VMEM((tm_count * chunks * per_tm, piece, LANES), jnp.bfloat16),
            pltpu.VMEM(tm_factor.shape, jnp.bfloat16),
            dma((chunks,)),
            dma((chunks,)),
            dma((chunks,)),
            dma((steps_all,)),
            dma((steps_all,)),
            dma((2,)),
            dma((steps_all,)),
            dma((tm_count * chunks * per_tm,)),
            dma,
            dma,
        ],
        compiler_params=pltpu.CompilerParams(
            collective_id=0, has_side_effects=True, vmem_limit_bytes=58 << 20
        ),
        cost_estimate=pl.CostEstimate(
            flops=2 * nodes * slab * (block * slots + tm_factor.shape[1]),
            bytes_accessed=2 * sp_blocks.size * chunks + 4 * field.size + 2 * tm_factor.size,
            transcendentals=0,
        ),
    )(field.reshape(blocks_dev, block, slab), sp_blocks, position, tm_factor)
    return out.reshape(rows)


def solution(mesh):
    in_specs = (P("space", "tm"), P("space", None, None, None), P("space", None), P("space"), P())
    out_specs = P(("space", "tm"))
    return jax.shard_map(
        on_device, mesh=mesh, in_specs=in_specs, out_specs=out_specs, check_vma=False
    )
```

time: 1240 us -> 199 us (0.16)
  waiting for transfers between devices: 1110 us -> 0 us
  Pallas kernels: 0 us -> 196 us
  matrix products: 45.7 us -> 0 us
  other arithmetic: 42.7 us -> 0.71 us
  local copies, waits for them, and re-layouts: 25.2 us -> 2.21 us
  between operations: 13.4 us -> 0.01 us
    reduce_scatter x1 -> x0, waiting for transfers between devices: 958 us -> none  [on_device(): lax.psum_scatter(jnp.dot(spatial_flat, own_rows, preferred_element_type=j...]
    pallas_call x0 -> x1, Pallas kernels: none -> 196 us  [on_device(): pl.pallas_call(functools.partial(kernel, (blocks_dev, slots, block, chunk...]
    ppermute x2 -> x0, waiting for transfers between devices: 156 us -> none  [the longest x1 154 us: extended(): lax.ppermute(tail, axis, [(i, (i + 1) % count) for i in range(count)])]
    dot_general x2 -> x0, matrix products: 45.7 us -> none  [the longest x1 23.5 us: on_device(): jnp.dot(spatial_flat, own_rows, preferred_element_type=jnp.float32)]
    concatenate x1 -> x0, other arithmetic: 34.4 us -> none  [extended(): jnp.concatenate([lax.ppermute(tail, axis, [(i, (i + 1) % count) for i in...]
    gather x1 -> x0, local copies, waits for them, and re-layouts: 24.8 us -> none  [on_device(): picked = jnp.take(padded_blocks, position, axis=0)]
  transfers between devices with their start and end apart: 3 -> 0, of which waited for: 3 -> 0; matrix products, arithmetic and copies ran while one was open for 0% -> 0% of each run, Pallas kernels for 0% -> 0%
where the time goes in v2:
time: 199 us
  Pallas kernels  196 us (98%)
  local copies, waits for them, and re-layouts  2.21 us (1%)
    pallas_call x1, Pallas kernels, on_device(): pl.pallas_call(functools.partial(kernel, (blocks_dev, slots, block, chunk...  196 us

profile of v2, /device:TPU:0, one launch (start us, length us, event | category | flops | bytes accessed | tf_op | source)
XLA Modules:
  0.0 199.1 jit_solution(9676934853789413236)
XLA Ops:
  0.0 0.7 fusion.1
  0.7 0.1 copy.6
  0.8 0.8 reshape.16.pos_ref
  1.6 196.2 %shard_map.55 = f32[28,128]{1,0:T(8,128)} custom-call(bf16[112,128,256]{2,1,0:T(8,128)(2,1)} %bitcast.3, bf16[112,5,128,128]{3,2,1,0:T(8,128)(2,1)} %blocks_ref.1, s32[560]{0:T(1024)} %reshape.16.pos_ref, bf16[1024,1024]{1,0:T(8,128)(2,1)} %factor_ref.1), custom_call_target="tpu_custom_call" | custom-call | flops 12213813248 | bytes 53477376 | tf_op jit(solution)/shard_map/pallas_call | solution.py:234
  197.8 1.3 copy.8
  (1 shorter events, 0.0 us)

commit v3 on v2

--- a/solution.py
+++ b/solution.py
@@ -8,8 +8,9 @@
 from jax.sharding import PartitionSpec as P
 
 LANES = 128
-PIECES = 8
-AHEAD = 3
+PIECES = 14
+AHEAD = 4
+LAG = 3
 MESH = pl.DeviceIdType.MESH
 
 
@@ -18,11 +19,10 @@
     near = scratch[:chunks]
     (land, blocks_buf, spatial, received, factor,
      own_sems, fast_send, fast_recv, slow_send, slow_recv,
-     blocks_sems, z_send, z_recv, local_sem, factor_sem) = scratch[chunks:]
+     blocks_sems, z_send, z_recv, factor_sem, shared, share_send, share_recv) = scratch[chunks:]
     piece_blocks = blocks_dev // PIECES
-    piece = piece_blocks * block
     steps_all = chunks * PIECES
-    per_tm = PIECES // tm_count
+    part = piece_blocks // tm_count
     slab = chunks * LANES
 
     place = lax.axis_index("space")
@@ -77,20 +77,75 @@
             blocks_ref.at[pl.ds(start, piece_blocks)], blocks_buf.at[slot], blocks_sems.at[slot]
         )
 
-    def target_of(g):
+    def place_of(source, c, p):
+        return (source * chunks + c) * PIECES + p
+
+    def z_copy(c, g, k):
+        p, target = ordered(g, odd, PIECES), lax.rem(me + k, tm_count)
+        return pltpu.make_async_remote_copy(
+            src_ref=spatial.at[c * PIECES + p, pl.ds(target * part, part)],
+            dst_ref=received.at[place_of(me, c, p)],
+            send_sem=z_send.at[(c * PIECES + g) * (tm_count - 1) + k - 1],
+            recv_sem=z_recv.at[place_of(me, c, p)],
+            device_id=(place, target),
+            device_id_type=MESH,
+        )
+
+    def z_arrival(c, g, k):
+        p, source = ordered(g, odd, PIECES), lax.rem(me + k, tm_count)
+        here = received.at[place_of(source, c, p)]
+        return pltpu.make_async_remote_copy(
+            src_ref=here,
+            dst_ref=here,
+            send_sem=z_send.at[0],
+            recv_sem=z_recv.at[place_of(source, c, p)],
+            device_id=(place, source),
+            device_id_type=MESH,
+        )
+
+    def share_copy(k):
+        return pltpu.make_async_remote_copy(
+            src_ref=shared.at[me],
+            dst_ref=shared.at[me],
+            send_sem=share_send.at[k - 1],
+            recv_sem=share_recv.at[me],
+            device_id=(place, lax.rem(me + k, tm_count)),
+            device_id_type=MESH,
+        )
+
+    def share_arrival(k):
+        source = lax.rem(me + k, tm_count)
+        return pltpu.make_async_remote_copy(
+            src_ref=shared.at[source],
+            dst_ref=shared.at[source],
+            send_sem=share_send.at[0],
+            recv_sem=share_recv.at[source],
+            device_id=(place, source),
+            device_id_type=MESH,
+        )
+
+    def score(g):
         p = ordered(g, odd, PIECES)
-        return p, p // per_tm, lax.rem(p, per_tm)
-
-    def z_copy(c, g):
-        p, target, half = target_of(g)
-        return pltpu.make_async_remote_copy(
-            src_ref=spatial.at[c * PIECES + p],
-            dst_ref=received.at[(me * chunks + c) * per_tm + half],
-            send_sem=z_send.at[c * PIECES + g],
-            recv_sem=z_recv.at[(me * chunks + c) * per_tm + half],
-            device_id=(place, target),
-            device_id_type=MESH,
-        )
+        width = factor.shape[0]
+        for c in range(chunks):
+            for k in range(1, tm_count):
+                z_arrival(c, g, k).wait_recv()
+        total = None
+        for source in range(tm_count):
+            cells = jnp.concatenate(
+                [received[place_of(source, c, p)].reshape(part * block, LANES) for c in range(chunks)], axis=1
+            )
+            product = jnp.dot(
+                cells, factor[source * slab : (source + 1) * slab, :], preferred_element_type=jnp.float32
+            )
+            total = product if total is None else total + product
+        square = total * total
+        folded = square[:, :LANES]
+        for c in range(1, width // LANES):
+            folded = folded + square[:, c * LANES : (c + 1) * LANES]
+        for j in range(part):
+            column = jnp.sum(folded[j * block : (j + 1) * block, :].T, axis=0, keepdims=True)
+            shared[me, pl.ds(p * part + j, 1), :] = column / width
 
     slow_copy(0).start()
     fast_copy(0).start()
@@ -112,7 +167,7 @@
 
         def stage(g, carry):
             n = c * PIECES + g
-            p, target, half = target_of(g)
+            p = ordered(g, odd, PIECES)
 
             @pl.when(n + 1 < steps_all)
             def _():
@@ -136,81 +191,56 @@
                 picked = jnp.concatenate(
                     [near[c][pos_ref[base + k]] for k in range(slots)], axis=0
                 )
-                spatial[c * PIECES + p, pl.ds(pl.multiple_of(i * block, block), block), :] = jnp.dot(
+                spatial[c * PIECES + p, i] = jnp.dot(
                     weights, picked, preferred_element_type=jnp.float32
                 ).astype(jnp.bfloat16)
                 return carry
 
             lax.fori_loop(0, piece_blocks, row, 0, unroll=2)
 
-            @pl.when(target != me)
-            def _():
-                z_copy(c, g).start()
-
-            @pl.when(target == me)
-            def _():
-                keep = pltpu.make_async_copy(
-                    spatial.at[c * PIECES + p], received.at[(me * chunks + c) * per_tm + half], local_sem
-                )
-                keep.start()
-                keep.wait()
+            for k in range(1, tm_count):
+                z_copy(c, g, k).start()
+            received[place_of(me, c, p)] = spatial[c * PIECES + p, pl.ds(me * part, part)]
+
+            if c + 1 == chunks:
+
+                @pl.when(g >= LAG)
+                def _():
+                    score(g - LAG)
 
             return carry
 
+        if c + 1 == chunks:
+            factor_copy.wait()
         lax.fori_loop(0, PIECES, stage, 0)
 
-    factor_copy.wait()
-    tile = 256
-    width = factor.shape[0]
-    for k in range(per_tm):
-        half = ordered(k, odd, per_tm)
-        for s in range(tm_count):
-
-            @pl.when(me != s)
-            def _():
-                for c in range(chunks):
-                    slot = (s * chunks + c) * per_tm + half
-                    pltpu.make_async_remote_copy(
-                        src_ref=received.at[slot],
-                        dst_ref=received.at[slot],
-                        send_sem=z_send.at[0],
-                        recv_sem=z_recv.at[slot],
-                        device_id=(place, s),
-                        device_id_type=MESH,
-                    ).wait_recv()
-
-        def score(t, carry):
-            rows = pl.ds(pl.multiple_of(t * tile, tile), tile)
-            total = None
-            for s in range(tm_count):
-                cells = jnp.concatenate(
-                    [received[(s * chunks + c) * per_tm + half, rows, :] for c in range(chunks)], axis=1
-                )
-                part = jnp.dot(cells, factor[s * slab : (s + 1) * slab, :], preferred_element_type=jnp.float32)
-                total = part if total is None else total + part
-            square = total * total
-            folded = square[:, :LANES]
-            for c in range(1, width // LANES):
-                folded = folded + square[:, c * LANES : (c + 1) * LANES]
-            for j in range(tile // LANES):
-                column = jnp.sum(folded[j * LANES : (j + 1) * LANES, :].T, axis=0, keepdims=True)
-                out_ref[pl.ds(half * (piece // LANES) + t * (tile // LANES) + j, 1), :] = column / width
+    def last(g, carry):
+        score(g)
+        return carry
+
+    lax.fori_loop(PIECES - LAG, PIECES, last, 0)
+    for k in range(1, tm_count):
+        share_copy(k).start()
+    for c in range(chunks):
+
+        def finish(g, carry):
+            for k in range(1, tm_count):
+                z_copy(c, g, k).wait_send()
             return carry
 
-        lax.fori_loop(0, piece // tile, score, 0)
-
-    for c in range(chunks):
-
-        def finish(g, carry):
-            _, target, _ = target_of(g)
-
-            @pl.when(target != me)
-            def _():
-                z_copy(c, g).wait_send()
-
-            return carry
-
         lax.fori_loop(0, PIECES, finish, 0)
+    for k in range(1, tm_count):
+        share_arrival(k).wait_recv()
+
+    def give(r, carry):
+        b = me * (blocks_dev // tm_count) + r
+        p, i = b // piece_blocks, lax.rem(b, piece_blocks)
+        out_ref[pl.ds(r, 1), :] = shared[i // part, pl.ds(p * part + lax.rem(i, part), 1), :]
+        return carry
+
+    lax.fori_loop(0, blocks_dev // tm_count, give, 0)
+    for k in range(1, tm_count):
+        share_copy(k).wait_send()
 
 
 def on_device(field, sp_blocks, sp_cols, sp_count, tm_factor):
@@ -225,9 +255,9 @@
     alive = jnp.arange(slots, dtype=jnp.int32)[None, :] < sp_count[:, None]
     position = jnp.where(alive, position, 3 * blocks_dev).reshape(-1)
 
-    piece = nodes // PIECES
+    piece_blocks = blocks_dev // PIECES
+    part = piece_blocks // tm_count
     rows = nodes // tm_count
-    per_tm = PIECES // tm_count
     steps_all = chunks * PIECES
     any_spec = pl.BlockSpec(memory_space=pl.ANY)
     dma = pltpu.SemaphoreType.DMA
@@ -238,10 +268,10 @@
         out_specs=pl.BlockSpec(memory_space=pltpu.VMEM),
         scratch_shapes=[pltpu.VMEM((3 * blocks_dev + 1, block, LANES), jnp.bfloat16) for _ in range(chunks)]
         + [
-            pltpu.VMEM((steps_all, piece // block, block, LANES), jnp.bfloat16),
-            pltpu.VMEM((2, blocks_dev // PIECES, slots, block, block), jnp.bfloat16),
-            pltpu.VMEM((steps_all, piece, LANES), jnp.bfloat16),
-            pltpu.VMEM((tm_count * chunks * per_tm, piece, LANES), jnp.bfloat16),
+            pltpu.VMEM((steps_all, piece_blocks, block, LANES), jnp.bfloat16),
+            pltpu.VMEM((2, piece_blocks, slots, block, block), jnp.bfloat16),
+            pltpu.VMEM((steps_all, piece_blocks, block, LANES), jnp.bfloat16),
+            pltpu.VMEM((tm_count * steps_all, part, block, LANES), jnp.bfloat16),
             pltpu.VMEM(tm_factor.shape, jnp.bfloat16),
             dma((chunks,)),
             dma((chunks,)),
@@ -249,10 +279,12 @@
             dma((steps_all,)),
             dma((steps_all,)),
             dma((2,)),
-            dma((steps_all,)),
-            dma((tm_count * chunks * per_tm,)),
+            dma((steps_all * (tm_count - 1),)),
+            dma((tm_count * steps_all,)),
             dma,
-            dma,
+            pltpu.VMEM((tm_count, PIECES * part, LANES), jnp.float32),
+            dma((tm_count - 1,)),
+            dma((tm_count,)),
         ],
         compiler_params=pltpu.CompilerParams(
             collective_id=0, has_side_effects=True, vmem_limit_bytes=58 << 20

time: 199 us -> 185 us (0.930)
  Pallas kernels: 196 us -> 182 us
    pallas_call x1, Pallas kernels: 196 us -> 182 us  [on_device(): pl.pallas_call(functools.partial(kernel, (blocks_dev, slots, block, chunk...]
where the time goes in v3:
time: 185 us
  Pallas kernels  182 us (98%)
  local copies, waits for them, and re-layouts  2.21 us (1%)
    pallas_call x1, Pallas kernels, on_device(): pl.pallas_call(functools.partial(kernel, (blocks_dev, slots, block, chunk...  182 us

profile of v3, /device:TPU:0, one launch (start us, length us, event | category | flops | bytes accessed | tf_op | source)
XLA Modules:
  0.0 184.8 jit_solution(6921270141235227743)
XLA Ops:
  0.0 0.7 fusion.1
  0.7 0.1 copy.6
  0.8 0.8 reshape.16.pos_ref
  1.6 181.9 %shard_map.55 = f32[28,128]{1,0:T(8,128)} custom-call(bf16[112,128,256]{2,1,0:T(8,128)(2,1)} %bitcast.3, bf16[112,5,128,128]{3,2,1,0:T(8,128)(2,1)} %blocks_ref.1, s32[560]{0:T(1024)} %reshape.16.pos_ref, bf16[1024,1024]{1,0:T(8,128)(2,1)} %factor_ref.1), custom_call_target="tpu_custom_call" | custom-call | flops 12213813248 | bytes 53477376 | tf_op jit(solution)/shard_map/pallas_call | solution.py:264
  183.5 1.3 copy.8
  (1 shorter events, 0.0 us)
